TPU v7x, 256 devices: a whole 4x4x8 slice. The times are simulated.
256 devices in a mesh: leaf: 64 (over z, x, core), vec: 4 (over y).
Axes of the slice: x: 4, y: 4, z: 8, core: 2. Of those that a mesh axis runs over, the one named last changes fastest.
Arguments:
- vectors: bfloat16 [64, 524288], P('vec', 'leaf'), may hold values from -6 to 6
- points: float32 [3, 524288], P(None, ('leaf', 'vec')), may hold values from 0 to 1
- leaf_basis: bfloat16 [4096, 64, 128], P('leaf'), may hold values from -0.5 to 0.5
- local_transfer: bfloat16 [8192, 64, 64], P('leaf'), may hold values from -0.625 to 0.625
- local_coupling: bfloat16 [8192, 64, 64], P('leaf'), may hold values from -0.75 to 0.75
- upper_transfer: bfloat16 [64, 64, 64], replicated, may hold values from -0.625 to 0.625
- upper_coupling: bfloat16 [64, 64, 64], replicated, may hold values from -0.75 to 0.75
- far_anchor: int32 [16384, 1], P('leaf'), may hold values from 0 to 63; in each aligned block of 256 rows (0 to 255, 256 to 511, ...) at most 8 rows name the same one
- far_leaves: int32 [16384, 2], P('leaf'), may hold values from 0 to 63
- far_block: bfloat16 [16384, 64, 64], P('leaf'), may hold values from -0.5 to 0.5
- near_cols: int32 [4096, 8], P('leaf'), may hold values from 0 to 4095, as said below
Outputs:
- product: float32 [64, 524288], P('vec', 'leaf')
Inputs may be any that keep to these rules, and one draw needn't show every extreme that they name: near_cols[t, 0] = t, and every entry lies within 8 leaves of t. `far_anchor`: among the 256 rows of one index of leaf, no value is named more than 8 times, and in every draw some value is named exactly 8 times.
All inputs are finite; a program needn't handle non-finite values.
Results may differ from a plain program's by a relative error of at most 0.0075.
Values may be sent and summed in bfloat16 or wider, within the bound.
No kernel may reach another device: no remote copies, remote signals or barrier semaphores. Data moves between devices by JAX's collectives and lax.ppermute only.
A program may use at most 128 MiB of HBM per device.

v0:
```python
import jax
import jax.numpy as jnp
from jax import lax
from jax.sharding import PartitionSpec as P

REACH = 8
kernel_scale = 1.0 / 64.0
delta_sq = 0.0025


def swapped(block, axis, distance):
    count = lax.axis_size(axis)
    route = []
    for low in range(count):
        high = low | 1 << distance
        if high != low and high < count:
            route += [(low, high), (high, low)]
    return lax.ppermute(block, axis, route)


def with_halo(cells, sides, width):
    for axis, dim in sides:
        count = lax.axis_size(axis)
        ends = count - 1
        head = lax.slice_in_dim(cells, 0, width, axis=dim)
        tail = lax.slice_in_dim(cells, cells.shape[dim] - width, cells.shape[dim], axis=dim)
        cells = jnp.concatenate(
            [
                lax.ppermute(tail, axis, [(i, (i + 1) % count) for i in range(ends)]),
                cells,
                lax.ppermute(head, axis, [((i + 1) % count, i) for i in range(ends)]),
            ],
            axis=dim,
        )
    return cells


def pick_node(table, node):
    return lax.dynamic_index_in_dim(table, node, 0, keepdims=False)


def per_device(
    vectors,
    points,
    leaf_basis,
    local_transfer,
    local_coupling,
    upper_transfer,
    upper_coupling,
    far_anchor,
    far_leaves,
    far_block,
    near_cols,
):
    highest = lax.Precision.HIGHEST
    vec_cols, point_count = vectors.shape
    leaf_dev, basis_rank, leaf_size = leaf_basis.shape
    n_leaf = lax.axis_size("leaf")
    top_depth = n_leaf.bit_length() - 1
    local_depth = leaf_dev.bit_length() - 1
    device = lax.axis_index("leaf")
    coords = lax.all_gather(points, "vec", axis=1, tiled=True)
    x_leaf = vectors.reshape(vec_cols, leaf_dev, leaf_size)
    coeff = jnp.einsum("vtp,tkp->tvk", x_leaf, leaf_basis, preferred_element_type=jnp.float32)
    transfer = local_transfer.astype(jnp.float32)
    coupling = local_coupling.astype(jnp.float32)
    upper_t = upper_transfer.astype(jnp.float32)
    upper_c = upper_coupling.astype(jnp.float32)
    levels = {local_depth: coeff}
    current = coeff
    for sub_depth in range(local_depth, 0, -1):
        node_count = 2**sub_depth
        product = jnp.einsum(
            "nvk,nkl->nvl", current, transfer[node_count : 2 * node_count], precision=highest
        )
        current = product.reshape(node_count // 2, 2, vec_cols, basis_rank).sum(1)
        levels[sub_depth - 1] = current
    root_coeff = current[0]
    root_share = jnp.dot(root_coeff, transfer[1], precision=highest)
    siblings = []
    carried = jnp.stack([root_coeff, root_share])
    for bit_pos in range(top_depth):
        partner = swapped(carried, "leaf", bit_pos)
        siblings.append(partner[0])
        if bit_pos + 1 < top_depth:
            node = jnp.right_shift(n_leaf + device, bit_pos + 1)
            parent = carried[1] + partner[1]
            carried = jnp.stack(
                [parent, jnp.dot(parent, pick_node(upper_t, node), precision=highest)]
            )
    downward = None
    for tree_depth in range(1, top_depth + 1):
        bit_pos = top_depth - tree_depth
        if bit_pos == 0:
            move_mat = transfer[1]
            pair_mat = coupling[1]
        else:
            node = jnp.right_shift(n_leaf + device, bit_pos)
            move_mat = pick_node(upper_t, node)
            pair_mat = pick_node(upper_c, node)
        coupled = jnp.dot(siblings[bit_pos], pair_mat, precision=highest)
        if downward is None:
            downward = coupled
        else:
            downward = jnp.dot(downward, move_mat.T, precision=highest) + coupled
    downward = downward[None]
    for sub_depth in range(1, local_depth + 1):
        node_count = 2**sub_depth
        coeffs = levels[sub_depth]
        sibling = coeffs.reshape(node_count // 2, 2, vec_cols, basis_rank)[:, ::-1].reshape(
            node_count, vec_cols, basis_rank
        )
        parent = jnp.repeat(downward, 2, axis=0)
        moved = jnp.einsum(
            "nvl,nkl->nvk", parent, transfer[node_count : 2 * node_count], precision=highest
        )
        downward = moved + jnp.einsum(
            "nvk,nkl->nvl", sibling, coupling[node_count : 2 * node_count], precision=highest
        )
    sent = coeff.astype(jnp.bfloat16)
    anchor = far_anchor[:, 0]
    source_local = far_leaves[:, 0]
    target_local = far_leaves[:, 1]
    everything = lax.all_gather(sent, "leaf", axis=0, tiled=True)
    fetched = jnp.take(everything, anchor * leaf_dev + source_local, axis=0)
    contrib = jnp.einsum("pvk,pkl->pvl", fetched, far_block, preferred_element_type=jnp.float32)
    onehot = (target_local[:, None] == jnp.arange(leaf_dev, dtype=jnp.int32)[None, :]).astype(
        jnp.float32
    )
    far_sum = jnp.einsum("pt,pvl->tvl", onehot, contrib, precision=highest)
    leaf_local = (downward + far_sum).astype(jnp.bfloat16)
    far_part = jnp.einsum(
        "tvk,tkp->vtp", leaf_local, leaf_basis, preferred_element_type=jnp.float32
    )
    padded_pts = with_halo(coords.astype(jnp.bfloat16), (("leaf", 1),), REACH * leaf_size).astype(
        coords.dtype
    )
    padded_vec = with_halo(vectors, (("leaf", 1),), REACH * leaf_size)
    block_count = leaf_dev + 2 * REACH
    pts_rows = jnp.transpose(padded_pts.reshape(3, block_count, leaf_size), (1, 0, 2))
    vec_rows = jnp.transpose(padded_vec.reshape(vec_cols, block_count, leaf_size), (1, 0, 2))
    own_rows = jnp.transpose(coords.reshape(3, leaf_dev, leaf_size), (1, 0, 2))
    local_cols = near_cols - device * leaf_dev + REACH
    group_size = min(8, leaf_dev)
    groups = leaf_dev // group_size

    def near_group(group, totals):
        first = group * group_size
        col_ids = lax.dynamic_slice_in_dim(local_cols, first, group_size, 0)
        targets = lax.dynamic_slice_in_dim(own_rows, first, group_size, 0)
        source = jnp.take(pts_rows, col_ids, axis=0)
        delta_x = targets[:, None, 0, :, None] - source[:, :, 0, None, :]
        delta_y = targets[:, None, 1, :, None] - source[:, :, 1, None, :]
        delta_z = targets[:, None, 2, :, None] - source[:, :, 2, None, :]
        dist_sq = delta_x * delta_x + delta_y * delta_y + delta_z * delta_z
        kernel = (kernel_scale * lax.rsqrt(dist_sq + delta_sq)).astype(jnp.bfloat16)
        values = jnp.take(vec_rows, col_ids, axis=0)
        block_sum = jnp.einsum("gkpq,gkvq->vgp", kernel, values, preferred_element_type=jnp.float32)
        return lax.dynamic_update_slice_in_dim(totals, block_sum, first, 1)

    near_sum = lax.fori_loop(
        0, groups, near_group, jnp.zeros((vec_cols, leaf_dev, leaf_size), jnp.float32)
    )
    return (near_sum + far_part).reshape(vec_cols, point_count)


def solution(mesh):
    return jax.shard_map(
        per_device,
        mesh=mesh,
        in_specs=(
            P("vec", "leaf"),
            P(None, ("leaf", "vec")),
            P("leaf", None, None),
            P("leaf", None, None),
            P("leaf", None, None),
            P(),
            P(),
            P("leaf", None),
            P("leaf", None),
            P("leaf", None, None),
            P("leaf", None),
        ),
        out_specs=P("vec", "leaf"),
        check_vma=False,
    )
```

profile of v0, /device:TPU:4, one launch (start us, length us, event | category | flops | bytes accessed | tf_op | source)
XLA Modules:
  0.0 243.2 jit_solution(12452155980335670206)
XLA Ops:
  6.5 2.8 %slice.146 = bf16[64,64,64]{0,2,1:T(8,128)(2,1)} slice(bf16[128,64,64]{0,2,1:T(8,128)(2,1)} %param.16), slice={[64:128], [0:64], [0:64]} | slice | bytes 1048576 | tf_op jit(solution)/shard_map/slice | solution.py:74
  9.3 2.6 %slice.147 = bf16[32,64,64]{0,2,1:T(8,128)(2,1)} slice(bf16[128,64,64]{0,2,1:T(8,128)(2,1)} %param.16), slice={[32:64], [0:64], [0:64]} | slice | bytes 524288 | tf_op jit(solution)/shard_map/slice | solution.py:74
  17.9 2.6 %copy.89 = bf16[64,64,64]{2,1,0:T(8,128)(2,1)S(1)} copy(bf16[64,64,64]{0,2,1:T(8,128)(2,1)} %slice.146) | data formatting | bytes 1048576
  20.5 2.8 %copy.90 = bf16[32,64,64]{2,1,0:T(8,128)(2,1)} copy(bf16[32,64,64]{0,2,1:T(8,128)(2,1)} %slice.147) | data formatting | bytes 524288
  40.1 12.7 %all_gather.6 = f32[3,8192]{1,0:T(4,128)S(1)} all-gather(f32[3,2048]{1,0:T(4,128)} %param.14), channel_id=1, replica_groups=mesh['leaf'=64,'vec'=4] {'vec'}, dimensions={1}, use_global_device_ids=true | all-gather | bytes 122880 | tf_op jit(solution)/shard_map/all_gather | solution.py:62
  56.6 3.6 %collective-permute-start.3 = (bf16[3,1024]{1,0:T(4,128)(2,1)}, bf16[3,1024]{1,0:T(4,128)(2,1)}, u32[]{:S(2)}, u32[]{:S(2)}) collective-permute-start(bf16[3,1024]{1,0:T(4,128)(2,1)} %get-tuple-element.156), channel_id=1, source_target_pairs={{4,0},{8,4},{12,8},{16,12},{20,16},{24,20},{28,24},{32,28},{36,32}... | collective-permute-start | bytes 18440 | tf_op jit(solution)/shard_map/ppermute | solution.py:31
  63.6 3.6 %collective-permute-start.1 = (bf16[16,1024]{1,0:T(8,128)(2,1)}, bf16[16,1024]{1,0:T(8,128)(2,1)}, u32[]{:S(2)}, u32[]{:S(2)}) collective-permute-start(bf16[16,1024]{1,0:T(8,128)(2,1)} %get-tuple-element.154), channel_id=1, source_target_pairs={{4,0},{8,4},{12,8},{16,12},{20,16},{24,20},{28,24},{32,28},{36,32}... | collective-permute-start | bytes 98312 | tf_op jit(solution)/shard_map/ppermute | solution.py:31
  105.3 2.8 %copy.101 = bf16[32,64,64]{2,1,0:T(8,128)(2,1)} copy(bf16[32,64,64]{0,2,1:T(8,128)(2,1)} %slice.169) | data formatting | bytes 524288
  108.1 7.5 %copy.83 = bf16[256,64,64]{2,1,0:T(8,128)(2,1)} copy(bf16[256,64,64]{0,2,1:T(8,128)(2,1)} %param.22) | data formatting | bytes 4194304 | tf_op args[9]
  116.4 3.3 %copy.102 = bf16[64,64,64]{2,1,0:T(8,128)(2,1)} copy(bf16[64,64,64]{0,2,1:T(8,128)(2,1)} %slice.170) | data formatting | bytes 1048576
  122.0 6.8 %collective-permute-start.7 = (f32[2,16,64]{2,1,0:T(8,128)S(1)}, f32[2,16,64]{2,1,0:T(8,128)S(1)}, u32[]{:S(2)}, u32[]{:S(2)}) collective-permute-start(f32[2,16,64]{2,1,0:T(8,128)S(1)} %pad_maximum_fusion.3), channel_id=1, source_target_pairs={{0,32},{32,0},{4,36},{36,4},{8,40},{40,8},{12,44},{44,12},{16,48},... | collective-permute-start | bytes 24584 | tf_op jit(solution)/shard_map/ppermute | solution.py:18
  131.7 3.6 %collective-permute-start.8 = (f32[2,16,64]{2,1,0:T(8,128)S(1)}, f32[2,16,64]{2,1,0:T(8,128)S(1)}, u32[]{:S(2)}, u32[]{:S(2)}) collective-permute-start(f32[2,16,64]{2,1,0:T(8,128)S(1)} %pad_maximum_fusion.4), channel_id=1, source_target_pairs={{0,64},{64,0},{4,68},{68,4},{8,72},{72,8},{12,76},{76,12},{16,80},... | collective-permute-start | bytes 24584 | tf_op jit(solution)/shard_map/ppermute | solution.py:18
  138.8 9.0 %collective-permute-start.9 = (f32[2,16,64]{2,1,0:T(8,128)}, f32[2,16,64]{2,1,0:T(8,128)}, u32[]{:S(2)}, u32[]{:S(2)}) collective-permute-start(f32[2,16,64]{2,1,0:T(8,128)} %pad_maximum_fusion.5), channel_id=1, source_target_pairs={{0,128},{128,0},{4,132},{132,4},{8,136},{136,8},{12,140},{140,12},... | collective-permute-start | bytes 24584 | tf_op jit(solution)/shard_map/ppermute | solution.py:18
  148.6 51.6 %while.13 = (s32[]{:T(128)}, f32[16,64,128]{2,0,1:T(8,128)}, s32[64,8]{0,1:T(8,128)S(1)}, bf16[80,16,128]{2,1,0:T(8,128)(2,1)S(1)}, f32[64,3,128]{2,0,1:T(8,128)...) while((s32[]{:T(128)}, f32[16,64,128]{2,0,1:T(8,128)}, ...), condition=%wide.region_1.0_spmd, body=%wide.region_0.0_spmd.sunk | while | flops 45246024 | bytes 1584527 | solution.py:161
  151.7 3.4 %fusion.160 = f32[16,64,128]{2,0,1:T(8,128)} fusion(f32[16,64,128]{2,0,1:T(8,128)} %get-tuple-element.221, s32[]{:T(128)S(6)} %select_n.98, f32[8,8,128]{2,1,0:T(8,128)} %bitcast.277, f32[8,128]{1,0:T(8,128)S(1)} %get-tuple-element.203, f32[8,8,128]{2,1,0:T(8,128)} %bitcast.278, f32[8,128]{1,0:T(8,128)S(1)} %get-tuple-element.205, ...), kind=kOutput, calls=%fused_computation.6.clone.1 | convolution fusion | flops 45219840 | bytes 438340 | tf_op jit(solution)/shard_map/while/body/eval_jaxpr/gkpq,gkvq->vgp/dot_general | solution.py:158
  158.1 3.4 %fusion.160 = f32[16,64,128]{2,0,1:T(8,128)} fusion(f32[16,64,128]{2,0,1:T(8,128)} %get-tuple-element.221, s32[]{:T(128)S(6)} %select_n.98, f32[8,8,128]{2,1,0:T(8,128)} %bitcast.277, f32[8,128]{1,0:T(8,128)S(1)} %get-tuple-element.203, f32[8,8,128]{2,1,0:T(8,128)} %bitcast.278, f32[8,128]{1,0:T(8,128)S(1)} %get-tuple-element.205, ...), kind=kOutput, calls=%fused_computation.6.clone.1 | convolution fusion | flops 45219840 | bytes 438340 | tf_op jit(solution)/shard_map/while/body/eval_jaxpr/gkpq,gkvq->vgp/dot_general | solution.py:158
  164.6 3.4 %fusion.160 = f32[16,64,128]{2,0,1:T(8,128)} fusion(f32[16,64,128]{2,0,1:T(8,128)} %get-tuple-element.221, s32[]{:T(128)S(6)} %select_n.98, f32[8,8,128]{2,1,0:T(8,128)} %bitcast.277, f32[8,128]{1,0:T(8,128)S(1)} %get-tuple-element.203, f32[8,8,128]{2,1,0:T(8,128)} %bitcast.278, f32[8,128]{1,0:T(8,128)S(1)} %get-tuple-element.205, ...), kind=kOutput, calls=%fused_computation.6.clone.1 | convolution fusion | flops 45219840 | bytes 438340 | tf_op jit(solution)/shard_map/while/body/eval_jaxpr/gkpq,gkvq->vgp/dot_general | solution.py:158
  171.0 3.4 %fusion.160 = f32[16,64,128]{2,0,1:T(8,128)} fusion(f32[16,64,128]{2,0,1:T(8,128)} %get-tuple-element.221, s32[]{:T(128)S(6)} %select_n.98, f32[8,8,128]{2,1,0:T(8,128)} %bitcast.277, f32[8,128]{1,0:T(8,128)S(1)} %get-tuple-element.203, f32[8,8,128]{2,1,0:T(8,128)} %bitcast.278, f32[8,128]{1,0:T(8,128)S(1)} %get-tuple-element.205, ...), kind=kOutput, calls=%fused_computation.6.clone.1 | convolution fusion | flops 45219840 | bytes 438340 | tf_op jit(solution)/shard_map/while/body/eval_jaxpr/gkpq,gkvq->vgp/dot_general | solution.py:158
  177.5 3.4 %fusion.160 = f32[16,64,128]{2,0,1:T(8,128)} fusion(f32[16,64,128]{2,0,1:T(8,128)} %get-tuple-element.221, s32[]{:T(128)S(6)} %select_n.98, f32[8,8,128]{2,1,0:T(8,128)} %bitcast.277, f32[8,128]{1,0:T(8,128)S(1)} %get-tuple-element.203, f32[8,8,128]{2,1,0:T(8,128)} %bitcast.278, f32[8,128]{1,0:T(8,128)S(1)} %get-tuple-element.205, ...), kind=kOutput, calls=%fused_computation.6.clone.1 | convolution fusion | flops 45219840 | bytes 438340 | tf_op jit(solution)/shard_map/while/body/eval_jaxpr/gkpq,gkvq->vgp/dot_general | solution.py:158
  184.0 3.4 %fusion.160 = f32[16,64,128]{2,0,1:T(8,128)} fusion(f32[16,64,128]{2,0,1:T(8,128)} %get-tuple-element.221, s32[]{:T(128)S(6)} %select_n.98, f32[8,8,128]{2,1,0:T(8,128)} %bitcast.277, f32[8,128]{1,0:T(8,128)S(1)} %get-tuple-element.203, f32[8,8,128]{2,1,0:T(8,128)} %bitcast.278, f32[8,128]{1,0:T(8,128)S(1)} %get-tuple-element.205, ...), kind=kOutput, calls=%fused_computation.6.clone.1 | convolution fusion | flops 45219840 | bytes 438340 | tf_op jit(solution)/shard_map/while/body/eval_jaxpr/gkpq,gkvq->vgp/dot_general | solution.py:158
  190.4 3.4 %fusion.160 = f32[16,64,128]{2,0,1:T(8,128)} fusion(f32[16,64,128]{2,0,1:T(8,128)} %get-tuple-element.221, s32[]{:T(128)S(6)} %select_n.98, f32[8,8,128]{2,1,0:T(8,128)} %bitcast.277, f32[8,128]{1,0:T(8,128)S(1)} %get-tuple-element.203, f32[8,8,128]{2,1,0:T(8,128)} %bitcast.278, f32[8,128]{1,0:T(8,128)S(1)} %get-tuple-element.205, ...), kind=kOutput, calls=%fused_computation.6.clone.1 | convolution fusion | flops 45219840 | bytes 438340 | tf_op jit(solution)/shard_map/while/body/eval_jaxpr/gkpq,gkvq->vgp/dot_general | solution.py:158
  196.8 3.4 %fusion.160 = f32[16,64,128]{2,0,1:T(8,128)} fusion(f32[16,64,128]{2,0,1:T(8,128)} %get-tuple-element.221, s32[]{:T(128)S(6)} %select_n.98, f32[8,8,128]{2,1,0:T(8,128)} %bitcast.277, f32[8,128]{1,0:T(8,128)S(1)} %get-tuple-element.203, f32[8,8,128]{2,1,0:T(8,128)} %bitcast.278, f32[8,128]{1,0:T(8,128)S(1)} %get-tuple-element.205, ...), kind=kOutput, calls=%fused_computation.6.clone.1 | convolution fusion | flops 45219840 | bytes 438340 | tf_op jit(solution)/shard_map/while/body/eval_jaxpr/gkpq,gkvq->vgp/dot_general | solution.py:158
  222.2 6.8 %gather_fusion.2 = bf16[256,16,64]{2,1,0:T(8,128)(2,1)S(1)} fusion(bf16[4096,16,64]{2,1,0:T(8,128)(2,1)} %all-gather.2.cloned.1.call-done, s32[1024]{0:T(1024)} %pad_clamp_fusion.1), kind=kCustom, calls=%fused_computation.2 | custom fusion | bytes 1049600 | tf_op jit(solution)/shard_map/jit(_take)/gather | solution.py:125
  229.0 3.6 %fusion.15 = f32[256,16,64]{2,1,0:T(8,128)S(1)} fusion(bf16[256,64,64]{2,1,0:T(8,128)(2,1)} %copy.83, bf16[256,16,64]{2,1,0:T(8,128)(2,1)S(1)} %gather_fusion.2, pred[256]{0:T(512)(128)(4,1)S(1)} %copy-done.36), kind=kOutput, calls=%fused_computation.40 | convolution fusion | flops 33816576 | bytes 3670272 | tf_op jit(solution)/shard_map/pvk,pkl->pvl/dot_general | solution.py:126
  (276 shorter events, 128.2 us)
Async XLA Ops:
  6.5 26.8 %copy-start = (bf16[64,64,128]{2,1,0:T(8,128)(2,1)S(1)}, bf16[64,64,128]{2,1,0:T(8,128)(2,1)}, u32[]{:S(2)}) copy-start(bf16[64,64,128]{2,1,0:T(8,128)(2,1)} %param.15) | copy-start | bytes 3145732
  6.5 215.7 %all-gather.2.cloned.1.call-start = ((), (), s32[]{:S(2)}) async-start(), calls=%async_computation | async-start | bytes 17039360 | tf_op jit(solution)/shard_map/all_gather | solution.py:124
  17.9 15.5 %copy-start.13 = (bf16[16,8192]{1,0:T(8,128)(2,1)S(1)}, bf16[16,8192]{1,0:T(8,128)(2,1)}, u32[]{:S(2)}) copy-start(bf16[16,8192]{1,0:T(8,128)(2,1)} %param.13) | copy-start | bytes 786436
  31.5 49.2 %copy-start.2 = (bf16[128,64,64]{0,2,1:T(8,128)(2,1)S(1)}, bf16[128,64,64]{0,2,1:T(8,128)(2,1)}, u32[]{:S(2)}) copy-start(bf16[128,64,64]{0,2,1:T(8,128)(2,1)} %param.17) | copy-start | bytes 3145732
  33.3 48.8 %copy-start.26 = (bf16[1,64,64]{2,1,0:T(8,128)(2,1)}, bf16[1,64,64]{2,1,0:T(8,128)(2,1)S(1)}, u32[]{:S(2)}) copy-start(bf16[1,64,64]{2,1,0:T(8,128)(2,1)S(1)} %copy.95) | copy-start | bytes 24580
  40.1 28.5 %collective-permute-start.4 = (f32[2,16,64]{2,1,0:T(8,128)}, f32[2,16,64]{2,1,0:T(8,128)}, u32[]{:S(2)}, u32[]{:S(2)}) collective-permute-start(f32[2,16,64]{2,1,0:T(8,128)} %pad_maximum_fusion), channel_id=1, source_target_pairs={{0,4},{4,0},{8,12},{12,8},{16,20},{20,16},{24,28},{28,24},{32,36},... | collective-permute-start | bytes 24584 | tf_op jit(solution)/shard_map/ppermute | solution.py:18
  54.7 74.0 %collective-permute-start.2 = (bf16[3,1024]{1,0:T(4,128)(2,1)}, bf16[3,1024]{1,0:T(4,128)(2,1)}, u32[]{:S(2)}, u32[]{:S(2)}) collective-permute-start(bf16[3,1024]{1,0:T(4,128)(2,1)} %get-tuple-element.155), channel_id=1, source_target_pairs={{0,4},{4,8},{8,12},{12,16},{16,20},{20,24},{24,28},{28,32},{32,36}... | collective-permute-start | bytes 18440 | tf_op jit(solution)/shard_map/ppermute | solution.py:29
  56.6 72.1 %collective-permute-start.3 = (bf16[3,1024]{1,0:T(4,128)(2,1)}, bf16[3,1024]{1,0:T(4,128)(2,1)}, u32[]{:S(2)}, u32[]{:S(2)}) collective-permute-start(bf16[3,1024]{1,0:T(4,128)(2,1)} %get-tuple-element.156), channel_id=1, source_target_pairs={{4,0},{8,4},{12,8},{16,12},{20,16},{24,20},{28,24},{32,28},{36,32}... | collective-permute-start | bytes 18440 | tf_op jit(solution)/shard_map/ppermute | solution.py:31
  61.7 73.6 %collective-permute-start = (bf16[16,1024]{1,0:T(8,128)(2,1)}, bf16[16,1024]{1,0:T(8,128)(2,1)}, u32[]{:S(2)}, u32[]{:S(2)}) collective-permute-start(bf16[16,1024]{1,0:T(8,128)(2,1)} %get-tuple-element.153), channel_id=1, source_target_pairs={{0,4},{4,8},{8,12},{12,16},{16,20},{20,24},{24,28},{28,32},{32,36}... | collective-permute-start | bytes 98312 | tf_op jit(solution)/shard_map/ppermute | solution.py:29
  63.6 71.6 %collective-permute-start.1 = (bf16[16,1024]{1,0:T(8,128)(2,1)}, bf16[16,1024]{1,0:T(8,128)(2,1)}, u32[]{:S(2)}, u32[]{:S(2)}) collective-permute-start(bf16[16,1024]{1,0:T(8,128)(2,1)} %get-tuple-element.154), channel_id=1, source_target_pairs={{4,0},{8,4},{12,8},{16,12},{20,16},{24,20},{28,24},{32,28},{36,32}... | collective-permute-start | bytes 98312 | tf_op jit(solution)/shard_map/ppermute | solution.py:31
  71.4 4.1 %collective-permute-start.5 = (f32[2,16,64]{2,1,0:T(8,128)}, f32[2,16,64]{2,1,0:T(8,128)}, u32[]{:S(2)}, u32[]{:S(2)}) collective-permute-start(f32[2,16,64]{2,1,0:T(8,128)} %pad_maximum_fusion.1), channel_id=1, source_target_pairs={{0,8},{8,0},{4,12},{12,4},{16,24},{24,16},{20,28},{28,20},{32,40},... | collective-permute-start | bytes 24584 | tf_op jit(solution)/shard_map/ppermute | solution.py:18
  78.2 42.2 %collective-permute-start.6 = (f32[2,16,64]{2,1,0:T(8,128)}, f32[2,16,64]{2,1,0:T(8,128)}, u32[]{:S(2)}, u32[]{:S(2)}) collective-permute-start(f32[2,16,64]{2,1,0:T(8,128)} %pad_maximum_fusion.2), channel_id=1, source_target_pairs={{0,16},{16,0},{4,20},{20,4},{8,24},{24,8},{12,28},{28,12},{32,48},... | collective-permute-start | bytes 24584 | tf_op jit(solution)/shard_map/ppermute | solution.py:18
  90.5 12.8 %copy-start.7 = (bf16[16,64,64]{0,2,1:T(8,128)(2,1)S(1)}, bf16[16,64,64]{0,2,1:T(8,128)(2,1)}, u32[]{:S(2)}) copy-start(bf16[16,64,64]{0,2,1:T(8,128)(2,1)} %slice.168) | copy-start | bytes 393220
  108.1 12.3 %copy-start.30 = (f32[16,64]{1,0:T(8,128)S(1)}, f32[16,64]{1,0:T(8,128)}, u32[]{:S(2)}) copy-start(f32[16,64]{1,0:T(8,128)} %copy-done.29) | copy-start | bytes 12292
  108.1 20.7 %copy-start.23 = (bf16[3,8192]{1,0:T(4,128)(2,1)S(1)}, bf16[3,8192]{1,0:T(4,128)(2,1)}, u32[]{:S(2)}) copy-start(bf16[3,8192]{1,0:T(4,128)(2,1)} %copy-done.22) | copy-start | bytes 147460
  108.1 27.2 %copy-start.14 = (bf16[16,8192]{1,0:T(8,128)(2,1)S(1)}, bf16[16,8192]{1,0:T(8,128)(2,1)}, u32[]{:S(2)}) copy-start(bf16[16,8192]{1,0:T(8,128)(2,1)} %param.13) | copy-start | bytes 786436
  115.6 33.0 %copy-start.28 = (s32[64,8]{0,1:T(8,128)S(1)}, s32[64,8]{0,1:T(8,128)}, u32[]{:S(2)}) copy-start(s32[64,8]{0,1:T(8,128)} %subtract_add_fusion) | copy-start | bytes 6148
  122.0 8.8 %collective-permute-start.7 = (f32[2,16,64]{2,1,0:T(8,128)S(1)}, f32[2,16,64]{2,1,0:T(8,128)S(1)}, u32[]{:S(2)}, u32[]{:S(2)}) collective-permute-start(f32[2,16,64]{2,1,0:T(8,128)S(1)} %pad_maximum_fusion.3), channel_id=1, source_target_pairs={{0,32},{32,0},{4,36},{36,4},{8,40},{40,8},{12,44},{44,12},{16,48},... | collective-permute-start | bytes 24584 | tf_op jit(solution)/shard_map/ppermute | solution.py:18
  131.7 5.6 %collective-permute-start.8 = (f32[2,16,64]{2,1,0:T(8,128)S(1)}, f32[2,16,64]{2,1,0:T(8,128)S(1)}, u32[]{:S(2)}, u32[]{:S(2)}) collective-permute-start(f32[2,16,64]{2,1,0:T(8,128)S(1)} %pad_maximum_fusion.4), channel_id=1, source_target_pairs={{0,64},{64,0},{4,68},{68,4},{8,72},{72,8},{12,76},{76,12},{16,80},... | collective-permute-start | bytes 24584 | tf_op jit(solution)/shard_map/ppermute | solution.py:18
  138.8 61.5 %collective-permute-start.9 = (f32[2,16,64]{2,1,0:T(8,128)}, f32[2,16,64]{2,1,0:T(8,128)}, u32[]{:S(2)}, u32[]{:S(2)}) collective-permute-start(f32[2,16,64]{2,1,0:T(8,128)} %pad_maximum_fusion.5), channel_id=1, source_target_pairs={{0,128},{128,0},{4,132},{132,4},{8,136},{136,8},{12,140},{140,12},... | collective-permute-start | bytes 24584 | tf_op jit(solution)/shard_map/ppermute | solution.py:18
  148.6 65.2 %copy-start.16 = (bf16[8,64,64]{2,1,0:T(8,128)(2,1)S(1)}, bf16[8,64,64]{2,1,0:T(8,128)(2,1)}, u32[]{:S(2)}) copy-start(bf16[8,64,64]{2,1,0:T(8,128)(2,1)} %copy.92) | copy-start | bytes 196612
  148.6 69.6 %copy-start.4 = (bf16[32,64,64]{2,1,0:T(8,128)(2,1)S(1)}, bf16[32,64,64]{2,1,0:T(8,128)(2,1)}, u32[]{:S(2)}) copy-start(bf16[32,64,64]{2,1,0:T(8,128)(2,1)} %copy.90) | copy-start | bytes 786436
  200.2 18.9 %copy-start.9 = (bf16[32,64,64]{2,1,0:T(8,128)(2,1)S(1)}, bf16[32,64,64]{2,1,0:T(8,128)(2,1)}, u32[]{:S(2)}) copy-start(bf16[32,64,64]{2,1,0:T(8,128)(2,1)} %copy.101) | copy-start | bytes 786436
  200.2 18.9 %copy-start.19 = (f32[16,2,16,64]{3,2,1,0:T(8,128)S(1)}, f32[16,2,16,64]{3,2,1,0:T(8,128)}, u32[]{:S(2)}) copy-start(f32[16,2,16,64]{3,2,1,0:T(8,128)} %rev.19) | copy-start | bytes 393220
  (24 other events, 102.0 us)
Sparse Core Ops, SparseCore 0:
  40.2 101.2 all-gather.1
where the time goes:
time: 247 us; the launch traced here: 243 us
  local copies, waits for them, and re-layouts  106 us (43%)
  matrix products  64.2 us (26%)
  starting transfers between devices  31.6 us (13%)
  between operations  13.8 us (6%)
  blocking collectives  12.7 us (5%)
  other arithmetic  11.6 us (5%)
  waiting for transfers between devices  3.48 us (1%)
    unnamed x91, local copies, waits for them, and re-layouts  44.2 us
    dot_general x8, matrix products, near_group(): jnp.einsum('gkpq,gkvq->vgp', kernel, values, preferred_element_type=jnp.f...  26.8 us
    ppermute x6, starting transfers between devices, swapped(): return lax.ppermute(block, axis, route)  20.5 us
    all_gather x1, blocking collectives, per_device(): coords = lax.all_gather(points, 'vec', axis=1, tiled=True)  12.7 us
    slice x6, local copies, waits for them, and re-layouts, per_device(): transfer[node_count:2 * node_count]  9.92 us
    slice x6, local copies, waits for them, and re-layouts, per_device(): coupling[node_count:2 * node_count]  8.36 us
    ppermute x2, starting transfers between devices, with_halo(): lax.ppermute(head, axis, [((i + 1) % count, i) for i in range(ends)])  7.29 us
    dot_general x6, matrix products, per_device(): jnp.einsum('nvl,nkl->nvk', parent, transfer[node_count:2 * node_count], p...  7.15 us
  transfers between devices with their start and end apart: 11, of which 3 were waited for; matrix products, arithmetic and copies ran while one was open for 54% of the time, Pallas kernels for 0%

commit v1 on v0

--- a/solution.py
+++ b/solution.py
@@ -59,7 +59,12 @@
     top_depth = n_leaf.bit_length() - 1
     local_depth = leaf_dev.bit_length() - 1
     device = lax.axis_index("leaf")
-    coords = lax.all_gather(points, "vec", axis=1, tiled=True)
+    ring = [points]
+    for hop in range(3):
+        ring.append(lax.ppermute(ring[-1], "vec", [(dev, (dev + 1) % 4) for dev in range(4)]))
+    coords = jnp.roll(
+        jnp.concatenate(ring[::-1], axis=1), (lax.axis_index("vec") + 1) * ring[0].shape[1], axis=1
+    )
     x_leaf = vectors.reshape(vec_cols, leaf_dev, leaf_size)
     coeff = jnp.einsum("vtp,tkp->tvk", x_leaf, leaf_basis, preferred_element_type=jnp.float32)
     transfer = local_transfer.astype(jnp.float32)

time: 247 us -> 224 us (0.907)
  the two profiles are of different devices: /device:TPU:4 before, /device:TPU:103 now
where the time goes in v1:
time: 224 us; the launch traced here: 221 us
  local copies, waits for them, and re-layouts  95 us (42%)
  matrix products  55.1 us (25%)
  starting transfers between devices  29.9 us (13%)
  waiting for transfers between devices  14 us (6%)
  between operations  13.9 us (6%)
  other arithmetic  13 us (6%)
    unnamed x105, local copies, waits for them, and re-layouts  45.3 us
    dot_general x8, matrix products, near_group(): jnp.einsum('gkpq,gkvq->vgp', kernel, values, preferred_element_type=jnp.f...  19.3 us
    ppermute x2, starting transfers between devices, with_halo(): lax.ppermute(tail, axis, [(i, (i + 1) % count) for i in range(ends)])  17.5 us
    slice x6, local copies, waits for them, and re-layouts, per_device(): transfer[node_count:2 * node_count]  9.88 us
    slice x6, local copies, waits for them, and re-layouts, per_device(): coupling[node_count:2 * node_count]  8.44 us
    ppermute x6, waiting for transfers between devices, swapped(): return lax.ppermute(block, axis, route)  7.56 us
    dot_general x6, matrix products, per_device(): jnp.einsum('nvl,nkl->nvk', parent, transfer[node_count:2 * node_count], p...  7.3 us
    gather x1, local copies, waits for them, and re-layouts, per_device(): fetched = jnp.take(everything, anchor * leaf_dev + source_local, axis=0)  6.95 us
  transfers between devices with their start and end apart: 14, of which 5 were waited for; matrix products, arithmetic and copies ran while one was open for 51% of the time, Pallas kernels for 0%

profile of v1, /device:TPU:103, one launch (start us, length us, event | category | flops | bytes accessed | tf_op | source)
XLA Modules:
  0.0 221.3 jit_solution(15229444463153597691)
XLA Ops:
  6.5 2.7 %slice.146 = bf16[64,64,64]{0,2,1:T(8,128)(2,1)} slice(bf16[128,64,64]{0,2,1:T(8,128)(2,1)} %param.16), slice={[64:128], [0:64], [0:64]} | slice | bytes 1048576 | tf_op jit(solution)/shard_map/slice | solution.py:79
  9.3 2.6 %slice.147 = bf16[32,64,64]{0,2,1:T(8,128)(2,1)} slice(bf16[128,64,64]{0,2,1:T(8,128)(2,1)} %param.16), slice={[32:64], [0:64], [0:64]} | slice | bytes 524288 | tf_op jit(solution)/shard_map/slice | solution.py:79
  17.8 2.6 %copy.89 = bf16[64,64,64]{2,1,0:T(8,128)(2,1)S(1)} copy(bf16[64,64,64]{0,2,1:T(8,128)(2,1)} %slice.146) | data formatting | bytes 1048576
  20.5 2.8 %copy.90 = bf16[32,64,64]{2,1,0:T(8,128)(2,1)} copy(bf16[32,64,64]{0,2,1:T(8,128)(2,1)} %slice.147) | data formatting | bytes 524288
  46.8 5.8 %collective-permute-start = (bf16[16,1024]{1,0:T(8,128)(2,1)}, bf16[16,1024]{1,0:T(8,128)(2,1)}, u32[]{:S(2)}, u32[]{:S(2)}) collective-permute-start(bf16[16,1024]{1,0:T(8,128)(2,1)} %get-tuple-element.153), channel_id=1, source_target_pairs={{0,4},{4,8},{8,12},{12,16},{16,20},{20,24},{24,28},{28,32},{32,36}... | collective-permute-start | bytes 98312 | tf_op jit(solution)/shard_map/ppermute | solution.py:29
  58.6 3.3 %collective-permute-done.9 = f32[2,16,64]{2,1,0:T(8,128)} collective-permute-done((f32[2,16,64]{2,1,0:T(8,128)}, f32[2,16,64]{2,1,0:T(8,128)}, u32[]{:S(2)}, u32[]{:S(2)}) %collective-permute-start.9) | collective-permute-done | bytes 8224 | tf_op jit(solution)/shard_map/ppermute | solution.py:18
  98.2 2.9 %copy.101 = bf16[32,64,64]{2,1,0:T(8,128)(2,1)} copy(bf16[32,64,64]{0,2,1:T(8,128)(2,1)} %slice.169) | data formatting | bytes 524288
  101.1 7.6 %copy.83 = bf16[256,64,64]{2,1,0:T(8,128)(2,1)} copy(bf16[256,64,64]{0,2,1:T(8,128)(2,1)} %param.22) | data formatting | bytes 4194304 | tf_op args[9]
  109.5 3.3 %copy.102 = bf16[64,64,64]{2,1,0:T(8,128)(2,1)} copy(bf16[64,64,64]{0,2,1:T(8,128)(2,1)} %slice.170) | data formatting | bytes 1048576
  115.8 3.2 %collective-permute-start.12 = (f32[2,16,64]{2,1,0:T(8,128)S(1)}, f32[2,16,64]{2,1,0:T(8,128)S(1)}, u32[]{:S(2)}, u32[]{:S(2)}) collective-permute-start(f32[2,16,64]{2,1,0:T(8,128)S(1)} %pad_maximum_fusion.5), channel_id=1, source_target_pairs={{0,128},{128,0},{4,132},{132,4},{8,136},{136,8},{12,140},{140,12},... | collective-permute-start | bytes 24584 | tf_op jit(solution)/shard_map/ppermute | solution.py:18
  119.9 2.5 %collective-permute-done.12 = f32[2,16,64]{2,1,0:T(8,128)S(1)} collective-permute-done((f32[2,16,64]{2,1,0:T(8,128)S(1)}, f32[2,16,64]{2,1,0:T(8,128)S(1)}, u32[]{:S(2)}, u32[]{:S(2)}) %collective-permute-start.12) | collective-permute-done | bytes 8224 | tf_op jit(solution)/shard_map/ppermute | solution.py:18
  141.7 2.6 %fusion.109 = f32[64,16,64]{2,1,0:T(8,128)} fusion(f32[64,16,64]{2,1,0:T(8,128)S(1)} %bitcast.271, bf16[64,64,64]{2,1,0:T(8,128)(2,1)S(1)} %copy.89), kind=kOutput, calls=%fused_computation.170 | convolution fusion | flops 50331648 | bytes 1048576 | tf_op jit(solution)/shard_map/nvl,nkl->nvk/dot_general | solution.py:119
  146.1 11.7 %collective-permute-start.5 = (bf16[3,1024]{1,0:T(4,128)(2,1)S(1)}, bf16[3,1024]{1,0:T(4,128)(2,1)S(1)}, u32[]{:S(2)}, u32[]{:S(2)}) collective-permute-start(bf16[3,1024]{1,0:T(4,128)(2,1)S(1)} %get-tuple-element.155), channel_id=1, source_target_pairs={{0,4},{4,8},{8,12},{12,16},{16,20},{20,24},{24,28},{28,32},{32,36}... | collective-permute-start | bytes 18440 | tf_op jit(solution)/shard_map/ppermute | solution.py:29
  159.8 6.3 %collective-permute-done.6 = bf16[3,1024]{1,0:T(4,128)(2,1)S(1)} collective-permute-done((bf16[3,1024]{1,0:T(4,128)(2,1)S(1)}, bf16[3,1024]{1,0:T(4,128)(2,1)S(1)}, u32[]{:S(2)}, u32[]{:S(2)}) %collective-permute-start.6) | collective-permute-done | bytes 6176 | tf_op jit(solution)/shard_map/ppermute | solution.py:31
  166.2 33.8 %while.13 = (s32[]{:T(128)}, f32[16,64,128]{2,0,1:T(8,128)S(1)}, s32[64,8]{0,1:T(8,128)S(1)}, bf16[80,16,128]{2,1,0:T(8,128)(2,1)S(1)}, f32[64,3,128]{2,0,1:T(8,...) while((s32[]{:T(128)}, f32[16,64,128]{2,0,1:T(8,128)S(1)}, ...), condition=%wide.region_1.2_spmd, body=%wide.region_0.1_spmd.sunk | while | flops 45246024 | bytes 1585487 | solution.py:166
  168.0 2.4 %fusion.160 = f32[16,64,128]{2,0,1:T(8,128)S(1)} fusion(f32[16,64,128]{2,0,1:T(8,128)S(1)} %get-tuple-element.221, s32[]{:T(128)S(6)} %select_n.113, f32[8,8,128]{2,1,0:T(8,128)S(1)} %bitcast.277, f32[8,128]{1,0:T(8,128)S(1)} %get-tuple-element.203, f32[8,8,128]{2,1,0:T(8,128)S(1)} %bitcast.278, f32[8,128]{1,0:T(8,128)S(1)} %get-tuple-element.205, ...), kind=kOutput, calls=%fused_computation.6.clone.1 | convolution fusion | flops 45219840 | bytes 439300 | tf_op jit(solution)/shard_map/while/body/eval_jaxpr/gkpq,gkvq->vgp/dot_general | solution.py:163
  172.3 2.4 %fusion.160 = f32[16,64,128]{2,0,1:T(8,128)S(1)} fusion(f32[16,64,128]{2,0,1:T(8,128)S(1)} %get-tuple-element.221, s32[]{:T(128)S(6)} %select_n.113, f32[8,8,128]{2,1,0:T(8,128)S(1)} %bitcast.277, f32[8,128]{1,0:T(8,128)S(1)} %get-tuple-element.203, f32[8,8,128]{2,1,0:T(8,128)S(1)} %bitcast.278, f32[8,128]{1,0:T(8,128)S(1)} %get-tuple-element.205, ...), kind=kOutput, calls=%fused_computation.6.clone.1 | convolution fusion | flops 45219840 | bytes 439300 | tf_op jit(solution)/shard_map/while/body/eval_jaxpr/gkpq,gkvq->vgp/dot_general | solution.py:163
  180.7 2.4 %fusion.160 = f32[16,64,128]{2,0,1:T(8,128)S(1)} fusion(f32[16,64,128]{2,0,1:T(8,128)S(1)} %get-tuple-element.221, s32[]{:T(128)S(6)} %select_n.113, f32[8,8,128]{2,1,0:T(8,128)S(1)} %bitcast.277, f32[8,128]{1,0:T(8,128)S(1)} %get-tuple-element.203, f32[8,8,128]{2,1,0:T(8,128)S(1)} %bitcast.278, f32[8,128]{1,0:T(8,128)S(1)} %get-tuple-element.205, ...), kind=kOutput, calls=%fused_computation.6.clone.1 | convolution fusion | flops 45219840 | bytes 439300 | tf_op jit(solution)/shard_map/while/body/eval_jaxpr/gkpq,gkvq->vgp/dot_general | solution.py:163
  184.9 2.4 %fusion.160 = f32[16,64,128]{2,0,1:T(8,128)S(1)} fusion(f32[16,64,128]{2,0,1:T(8,128)S(1)} %get-tuple-element.221, s32[]{:T(128)S(6)} %select_n.113, f32[8,8,128]{2,1,0:T(8,128)S(1)} %bitcast.277, f32[8,128]{1,0:T(8,128)S(1)} %get-tuple-element.203, f32[8,8,128]{2,1,0:T(8,128)S(1)} %bitcast.278, f32[8,128]{1,0:T(8,128)S(1)} %get-tuple-element.205, ...), kind=kOutput, calls=%fused_computation.6.clone.1 | convolution fusion | flops 45219840 | bytes 439300 | tf_op jit(solution)/shard_map/while/body/eval_jaxpr/gkpq,gkvq->vgp/dot_general | solution.py:163
  189.2 2.4 %fusion.160 = f32[16,64,128]{2,0,1:T(8,128)S(1)} fusion(f32[16,64,128]{2,0,1:T(8,128)S(1)} %get-tuple-element.221, s32[]{:T(128)S(6)} %select_n.113, f32[8,8,128]{2,1,0:T(8,128)S(1)} %bitcast.277, f32[8,128]{1,0:T(8,128)S(1)} %get-tuple-element.203, f32[8,8,128]{2,1,0:T(8,128)S(1)} %bitcast.278, f32[8,128]{1,0:T(8,128)S(1)} %get-tuple-element.205, ...), kind=kOutput, calls=%fused_computation.6.clone.1 | convolution fusion | flops 45219840 | bytes 439300 | tf_op jit(solution)/shard_map/while/body/eval_jaxpr/gkpq,gkvq->vgp/dot_general | solution.py:163
  193.4 2.4 %fusion.160 = f32[16,64,128]{2,0,1:T(8,128)S(1)} fusion(f32[16,64,128]{2,0,1:T(8,128)S(1)} %get-tuple-element.221, s32[]{:T(128)S(6)} %select_n.113, f32[8,8,128]{2,1,0:T(8,128)S(1)} %bitcast.277, f32[8,128]{1,0:T(8,128)S(1)} %get-tuple-element.203, f32[8,8,128]{2,1,0:T(8,128)S(1)} %bitcast.278, f32[8,128]{1,0:T(8,128)S(1)} %get-tuple-element.205, ...), kind=kOutput, calls=%fused_computation.6.clone.1 | convolution fusion | flops 45219840 | bytes 439300 | tf_op jit(solution)/shard_map/while/body/eval_jaxpr/gkpq,gkvq->vgp/dot_general | solution.py:163
  197.6 2.4 %fusion.160 = f32[16,64,128]{2,0,1:T(8,128)S(1)} fusion(f32[16,64,128]{2,0,1:T(8,128)S(1)} %get-tuple-element.221, s32[]{:T(128)S(6)} %select_n.113, f32[8,8,128]{2,1,0:T(8,128)S(1)} %bitcast.277, f32[8,128]{1,0:T(8,128)S(1)} %get-tuple-element.203, f32[8,8,128]{2,1,0:T(8,128)S(1)} %bitcast.278, f32[8,128]{1,0:T(8,128)S(1)} %get-tuple-element.205, ...), kind=kOutput, calls=%fused_computation.6.clone.1 | convolution fusion | flops 45219840 | bytes 439300 | tf_op jit(solution)/shard_map/while/body/eval_jaxpr/gkpq,gkvq->vgp/dot_general | solution.py:163
  200.0 7.0 %gather_fusion.2 = bf16[256,16,64]{2,1,0:T(8,128)(2,1)S(1)} fusion(bf16[4096,16,64]{2,1,0:T(8,128)(2,1)} %all-gather.2.cloned.1.call-done, s32[1024]{0:T(1024)} %pad_clamp_fusion.1), kind=kCustom, calls=%fused_computation.2 | custom fusion | bytes 1049600 | tf_op jit(solution)/shard_map/jit(_take)/gather | solution.py:130
  207.1 3.6 %fusion.15 = f32[256,16,64]{2,1,0:T(8,128)S(1)} fusion(bf16[256,64,64]{2,1,0:T(8,128)(2,1)} %copy.83, bf16[256,16,64]{2,1,0:T(8,128)(2,1)S(1)} %gather_fusion.2, pred[256]{0:T(512)(128)(4,1)S(1)} %copy-done.39), kind=kOutput, calls=%fused_computation.40 | convolution fusion | flops 33816576 | bytes 3670272 | tf_op jit(solution)/shard_map/pvk,pkl->pvl/dot_general | solution.py:131
  (296 shorter events, 119.6 us)
Async XLA Ops:
  6.5 26.7 %copy-start = (bf16[64,64,128]{2,1,0:T(8,128)(2,1)S(1)}, bf16[64,64,128]{2,1,0:T(8,128)(2,1)}, u32[]{:S(2)}) copy-start(bf16[64,64,128]{2,1,0:T(8,128)(2,1)} %param.15) | copy-start | bytes 3145732
  6.5 193.5 %all-gather.2.cloned.1.call-start = ((), (), s32[]{:S(2)}) async-start(), calls=%async_computation | async-start | bytes 17039360 | tf_op jit(solution)/shard_map/all_gather | solution.py:129
  29.1 44.5 %copy-start.2 = (bf16[128,64,64]{0,2,1:T(8,128)(2,1)S(1)}, bf16[128,64,64]{0,2,1:T(8,128)(2,1)}, u32[]{:S(2)}) copy-start(bf16[128,64,64]{0,2,1:T(8,128)(2,1)} %param.17) | copy-start | bytes 3145732
  35.6 42.3 %copy-start.9 = (f32[32,16,64]{2,1,0:T(8,128)}, f32[32,16,64]{2,1,0:T(8,128)S(1)}, u32[]{:S(2)}) copy-start(f32[32,16,64]{2,1,0:T(8,128)S(1)} %bitcast_reduce_fusion) | copy-start | bytes 393220
  40.0 2.1 collective-permute-start.7
  40.7 72.2 %collective-permute-start.2 = (f32[3,2048]{1,0:T(4,128)}, f32[3,2048]{1,0:T(4,128)}, u32[]{:S(2)}, u32[]{:S(2)}) collective-permute-start(f32[3,2048]{1,0:T(4,128)} %param.14), channel_id=1, source_target_pairs={{0,1},{1,2},{2,3},{3,0},{4,5},{5,6},{6,7},{7,4},{8,9},{9,10},{10,1... | collective-permute-start | bytes 73736 | tf_op jit(solution)/shard_map/ppermute | solution.py:64
  44.9 9.7 %collective-permute-start.8 = (f32[2,16,64]{2,1,0:T(8,128)}, f32[2,16,64]{2,1,0:T(8,128)}, u32[]{:S(2)}, u32[]{:S(2)}) collective-permute-start(f32[2,16,64]{2,1,0:T(8,128)} %pad_maximum_fusion.1), channel_id=1, source_target_pairs={{0,8},{8,0},{4,12},{12,4},{16,24},{24,16},{20,28},{28,20},{32,40},... | collective-permute-start | bytes 24584 | tf_op jit(solution)/shard_map/ppermute | solution.py:18
  46.8 72.2 %collective-permute-start = (bf16[16,1024]{1,0:T(8,128)(2,1)}, bf16[16,1024]{1,0:T(8,128)(2,1)}, u32[]{:S(2)}, u32[]{:S(2)}) collective-permute-start(bf16[16,1024]{1,0:T(8,128)(2,1)} %get-tuple-element.153), channel_id=1, source_target_pairs={{0,4},{4,8},{8,12},{12,16},{16,20},{20,24},{24,28},{28,32},{32,36}... | collective-permute-start | bytes 98312 | tf_op jit(solution)/shard_map/ppermute | solution.py:29
  52.6 66.4 %collective-permute-start.1 = (bf16[16,1024]{1,0:T(8,128)(2,1)}, bf16[16,1024]{1,0:T(8,128)(2,1)}, u32[]{:S(2)}, u32[]{:S(2)}) collective-permute-start(bf16[16,1024]{1,0:T(8,128)(2,1)} %get-tuple-element.154), channel_id=1, source_target_pairs={{4,0},{8,4},{12,8},{16,12},{20,16},{24,20},{28,24},{32,28},{36,32}... | collective-permute-start | bytes 98312 | tf_op jit(solution)/shard_map/ppermute | solution.py:31
  57.4 4.6 %collective-permute-start.9 = (f32[2,16,64]{2,1,0:T(8,128)}, f32[2,16,64]{2,1,0:T(8,128)}, u32[]{:S(2)}, u32[]{:S(2)}) collective-permute-start(f32[2,16,64]{2,1,0:T(8,128)} %pad_maximum_fusion.2), channel_id=1, source_target_pairs={{0,16},{16,0},{4,20},{20,4},{8,24},{24,8},{12,28},{28,12},{32,48},... | collective-permute-start | bytes 24584 | tf_op jit(solution)/shard_map/ppermute | solution.py:18
  64.7 3.5 %collective-permute-start.10 = (f32[2,16,64]{2,1,0:T(8,128)}, f32[2,16,64]{2,1,0:T(8,128)}, u32[]{:S(2)}, u32[]{:S(2)}) collective-permute-start(f32[2,16,64]{2,1,0:T(8,128)} %pad_maximum_fusion.3), channel_id=1, source_target_pairs={{0,32},{32,0},{4,36},{36,4},{8,40},{40,8},{12,44},{44,12},{16,48},... | collective-permute-start | bytes 24584 | tf_op jit(solution)/shard_map/ppermute | solution.py:18
  71.0 43.1 %collective-permute-start.11 = (f32[2,16,64]{2,1,0:T(8,128)}, f32[2,16,64]{2,1,0:T(8,128)}, u32[]{:S(2)}, u32[]{:S(2)}) collective-permute-start(f32[2,16,64]{2,1,0:T(8,128)} %pad_maximum_fusion.4), channel_id=1, source_target_pairs={{0,64},{64,0},{4,68},{68,4},{8,72},{72,8},{12,76},{76,12},{16,80},... | collective-permute-start | bytes 24584 | tf_op jit(solution)/shard_map/ppermute | solution.py:18
  108.7 30.0 %copy-start.4 = (bf16[32,64,64]{2,1,0:T(8,128)(2,1)S(1)}, bf16[32,64,64]{2,1,0:T(8,128)(2,1)}, u32[]{:S(2)}) copy-start(bf16[32,64,64]{2,1,0:T(8,128)(2,1)} %copy.90) | copy-start | bytes 786436
  109.5 30.1 %copy-start.10 = (bf16[32,64,64]{2,1,0:T(8,128)(2,1)S(1)}, bf16[32,64,64]{2,1,0:T(8,128)(2,1)}, u32[]{:S(2)}) copy-start(bf16[32,64,64]{2,1,0:T(8,128)(2,1)} %copy.101) | copy-start | bytes 786436
  112.9 25.4 %copy-start.19 = (bf16[16,64,64]{2,1,0:T(8,128)(2,1)S(1)}, bf16[16,64,64]{2,1,0:T(8,128)(2,1)}, u32[]{:S(2)}) copy-start(bf16[16,64,64]{2,1,0:T(8,128)(2,1)} %copy.100) | copy-start | bytes 393220
  112.9 25.5 %copy-start.24 = (f32[8,2,16,64]{3,2,1,0:T(8,128)S(1)}, f32[8,2,16,64]{3,2,1,0:T(8,128)}, u32[]{:S(2)}) copy-start(f32[8,2,16,64]{3,2,1,0:T(8,128)} %rev.18) | copy-start | bytes 196612
  112.9 26.7 %copy-start.18 = (f32[16,2,16,64]{3,2,1,0:T(8,128)S(1)}, f32[16,2,16,64]{3,2,1,0:T(8,128)}, u32[]{:S(2)}) copy-start(f32[16,2,16,64]{3,2,1,0:T(8,128)} %rev.19) | copy-start | bytes 393220
  112.9 27.3 %collective-permute-start.3 = (f32[3,2048]{1,0:T(4,128)}, f32[3,2048]{1,0:T(4,128)S(1)}, u32[]{:S(2)}, u32[]{:S(2)}) collective-permute-start(f32[3,2048]{1,0:T(4,128)} %collective-permute-done.2), channel_id=1, source_target_pairs={{0,1},{1,2},{2,3},{3,0},{4,5},{5,6},{6,7},{7,4},{8,9},{9,10},{10,1... | collective-permute-start | bytes 73736 | tf_op jit(solution)/shard_map/ppermute | solution.py:64
  115.8 6.7 %collective-permute-start.12 = (f32[2,16,64]{2,1,0:T(8,128)S(1)}, f32[2,16,64]{2,1,0:T(8,128)S(1)}, u32[]{:S(2)}, u32[]{:S(2)}) collective-permute-start(f32[2,16,64]{2,1,0:T(8,128)S(1)} %pad_maximum_fusion.5), channel_id=1, source_target_pairs={{0,128},{128,0},{4,132},{132,4},{8,136},{136,8},{12,140},{140,12},... | collective-permute-start | bytes 24584 | tf_op jit(solution)/shard_map/ppermute | solution.py:18
  138.3 27.9 %copy-start.29 = (s32[64,8]{0,1:T(8,128)S(1)}, s32[64,8]{0,1:T(8,128)}, u32[]{:S(2)}) copy-start(s32[64,8]{0,1:T(8,128)} %subtract_add_fusion) | copy-start | bytes 6148
  140.2 4.3 %collective-permute-start.4 = (f32[3,2048]{1,0:T(4,128)S(1)}, f32[3,2048]{1,0:T(4,128)S(1)}, u32[]{:S(2)}, u32[]{:S(2)}) collective-permute-start(f32[3,2048]{1,0:T(4,128)S(1)} %collective-permute-done.3), channel_id=1, source_target_pairs={{0,1},{1,2},{2,3},{3,0},{4,5},{5,6},{6,7},{7,4},{8,9},{9,10},{10,1... | collective-permute-start | bytes 73736 | tf_op jit(solution)/shard_map/ppermute | solution.py:64
  146.1 13.7 %collective-permute-start.5 = (bf16[3,1024]{1,0:T(4,128)(2,1)S(1)}, bf16[3,1024]{1,0:T(4,128)(2,1)S(1)}, u32[]{:S(2)}, u32[]{:S(2)}) collective-permute-start(bf16[3,1024]{1,0:T(4,128)(2,1)S(1)} %get-tuple-element.155), channel_id=1, source_target_pairs={{0,4},{4,8},{8,12},{12,16},{16,20},{20,24},{24,28},{28,32},{32,36}... | collective-permute-start | bytes 18440 | tf_op jit(solution)/shard_map/ppermute | solution.py:29
  157.8 8.3 %collective-permute-start.6 = (bf16[3,1024]{1,0:T(4,128)(2,1)S(1)}, bf16[3,1024]{1,0:T(4,128)(2,1)S(1)}, u32[]{:S(2)}, u32[]{:S(2)}) collective-permute-start(bf16[3,1024]{1,0:T(4,128)(2,1)S(1)} %get-tuple-element.156), channel_id=1, source_target_pairs={{4,0},{8,4},{12,8},{16,12},{20,16},{24,20},{28,24},{32,28},{36,32}... | collective-permute-start | bytes 18440 | tf_op jit(solution)/shard_map/ppermute | solution.py:31
  166.2 40.8 %copy-start.39 = (pred[256]{0:T(512)(128)(4,1)S(1)}, pred[256]{0:T(512)(128)(4,1)}, u32[]{:S(2)}) copy-start(pred[256]{0:T(512)(128)(4,1)} %get-tuple-element.145) | copy-start | bytes 772
  (30 other events, 190.7 us)
Sparse Core Ops, SparseCore 0:
  40.8 99.6 all-gather.1
